TPU v7x, 256 devices: a whole 4x4x8 slice. The times are simulated.
256 devices in a mesh: section: 8 (over z), expert: 16 (over y, x), dp: 2 (over core).
Axes of the slice: x: 4, y: 4, z: 8, core: 2. Of those that a mesh axis runs over, the one named last changes fastest.
Arguments:
- acts: bfloat16 [8, 3, 2048, 1024], P('section', None, ('expert', 'dp')), may hold values from -6 to 6
- out_grad: bfloat16 [3, 2048, 1024], P(None, ('expert', 'dp')), may hold values from -6 to 6
- ln_gain: float32 [8, 1024], P('section'), may hold values from 0.1 to 1.9
- router: bfloat16 [8, 1024, 16], P('section'), may hold values from -0.1875 to 0.1875
- w_in: bfloat16 [8, 16, 1024, 4096], P('section', 'expert', None, 'dp'), may hold values from -0.1875 to 0.1875
- w_out: bfloat16 [8, 16, 4096, 1024], P('section', 'expert', 'dp'), may hold values from -0.09375 to 0.09375
- expert_ids: int32 [8, 3, 2048, 2], P('section', None, ('expert', 'dp')), may hold values from 0 to 15, as said below
- slot_ids: int32 [8, 3, 2048, 2], P('section', None, ('expert', 'dp')), may hold values from 0 to 9, as said below
- capacity: int32 [8, 3, 16], P('section'), may hold values from 5 to 10
Outputs:
- in_grads: bfloat16 [8, 3, 2048, 1024], P('section', None, ('expert', 'dp'))
- gain_grad: float32 [8, 1024], P('section')
- router_grad: float32 [8, 1024, 16], P('section')
Inputs may be any that keep to these rules, and one draw needn't show every extreme that they name: `expert_ids`: A token's two experts differ. `slot_ids`: within one block, micro-batch and aligned block of 64 tokens (the tokens of one device), the choices that name one expert hold the slots 0, 1, 2, ... without gaps, at most 10 of them; in every block and micro-batch one expert has 10 choices from every aligned block and capacity 10.
All inputs are finite; a program needn't handle non-finite values.
Results may differ from a plain program's by a relative error of at most 0.03.
Values may be sent and summed in bfloat16 or wider, within the bound.
A program may use at most 128 MiB of HBM per device.

v0:
```python
import math
import jax
import jax.numpy as jnp
from jax import lax
from jax.sharding import PartitionSpec as P

GELU_C = math.sqrt(2.0 / math.pi)
PRECISE = lax.Precision.HIGHEST


def from_behind(shard, axis, by):
    count = lax.axis_size(axis)
    pairs = [(i, i + by) for i in range(count) if 0 <= i + by < count]
    return lax.ppermute(shard, axis, pairs)


def gelu_pair(hidden):
    inner_arg = GELU_C * (hidden + 0.044715 * hidden * hidden * hidden)
    tanh_val = jnp.tanh(inner_arg)
    active = 0.5 * hidden * (1.0 + tanh_val)
    gelu_slope = 0.5 * (1.0 + tanh_val) + 0.5 * hidden * (1.0 - tanh_val * tanh_val) * GELU_C * (
        1.0 + 3.0 * 0.044715 * hidden * hidden
    )
    return (active, gelu_slope)


def token_forward(inputs, norm_scale_weight, router_w):
    values = inputs.astype(jnp.float32)
    centred = values - jnp.mean(values, axis=-1, keepdims=True)
    inverse_deviation = lax.rsqrt(jnp.mean(centred * centred, axis=-1, keepdims=True) + 1e-06)
    expert_unit_rows = centred * inverse_deviation
    normed = (expert_unit_rows * norm_scale_weight).astype(jnp.bfloat16)
    logits = jnp.dot(normed, router_w, preferred_element_type=jnp.float32)
    return (expert_unit_rows, inverse_deviation, normed, logits)


def gate_pair(chosen):
    first_gate = 1.0 / (1.0 + jnp.exp(chosen[:, 1] - chosen[:, 0]))
    return jnp.stack([first_gate, 1.0 - first_gate], axis=1)


def token_backward(
    grad_out,
    expert_unit_rows,
    inverse_deviation,
    normed,
    norm_scale_weight,
    router_w,
    gate_vals,
    pick_table,
    gate_dots,
    expert_part,
):
    gate_diff = gate_vals[:, 0] * gate_vals[:, 1] * (gate_dots[:, 0] - gate_dots[:, 1])
    dlogits = gate_diff[:, None] * (pick_table[:, 0, :] - pick_table[:, 1, :])
    norm_gradient = expert_part + jnp.dot(
        dlogits, router_w.astype(jnp.float32).T, precision=PRECISE
    )
    router_term = jnp.dot(normed.astype(jnp.float32).T, dlogits, precision=PRECISE)
    gain_term = jnp.sum(norm_gradient * expert_unit_rows, axis=0)
    normalized_input_gradient = norm_gradient * norm_scale_weight
    input_gradient = inverse_deviation * (
        normalized_input_gradient
        - jnp.mean(normalized_input_gradient, axis=-1, keepdims=True)
        - expert_unit_rows
        * jnp.mean(normalized_input_gradient * expert_unit_rows, axis=-1, keepdims=True)
    )
    in_grad = (grad_out.astype(jnp.float32) + input_gradient).astype(jnp.bfloat16)
    return (in_grad, gain_term, router_term)


def expert_terms(rows_u, rows_grad, first_proj, second_proj):
    hidden = jnp.dot(rows_u, first_proj, preferred_element_type=jnp.float32)
    active, gelu_slope = gelu_pair(hidden)
    back_grad = lax.dot_general(
        rows_grad, second_proj, (((1,), (1,)), ((), ())), preferred_element_type=jnp.float32
    )
    gate_part = jnp.sum(active * back_grad, axis=-1)
    pre_grad = (back_grad * gelu_slope).astype(jnp.bfloat16)
    slot_part = lax.dot_general(
        pre_grad, first_proj, (((1,), (1,)), ((), ())), preferred_element_type=jnp.float32
    )
    return (slot_part, gate_part)


def per_device(acts, out_grad, ln_gain, router, w_in, w_out, expert_ids, slot_ids, capacity):
    section_count = lax.axis_size("section")
    section_index = lax.axis_index("section")
    microbatch_count = acts.shape[1]
    tok_rows = acts.shape[2]
    model_width = acts.shape[3]
    experts = router.shape[2]
    top_count = expert_ids.shape[3]
    cap_slots = 5 * tok_rows * top_count // (4 * experts)
    slot_count = experts * cap_slots
    tokens_all = tok_rows * lax.axis_size("expert") * lax.axis_size("dp")
    grad_scale = 1.0 / math.sqrt(microbatch_count * tokens_all)
    norm_scale_weight = ln_gain[0]
    router_w = router[0]
    first_proj = w_in[0, 0]
    second_proj = w_out[0, 0]
    positions = jnp.arange(slot_count, dtype=jnp.int32)
    columns = jnp.arange(experts, dtype=jnp.int32)
    section_acts = acts[0]
    section_ids = expert_ids[0]
    section_slots = slot_ids[0]
    section_caps = capacity[0]

    def run_experts(recv_u, recv_grad, is_valid):
        lead_rows = recv_u.shape[0]
        flat_u = recv_u.reshape(lead_rows * cap_slots, model_width)
        flat_grad = recv_grad.reshape(lead_rows * cap_slots, model_width)

        def expert_work(packed):
            return expert_terms(packed[0], packed[1], first_proj, second_proj)

        def skip_work(packed):
            return (
                jnp.zeros(packed[0].shape, jnp.float32),
                jnp.zeros(packed[0].shape[:1], jnp.float32),
            )

        slot_part, gate_part = lax.cond(is_valid, expert_work, skip_work, (flat_u, flat_grad))
        return (
            slot_part.reshape(lead_rows, cap_slots, model_width),
            gate_part.reshape(lead_rows, cap_slots),
        )

    def step_fn(step_index, loop_state):
        incoming, grads_acc, gain_acc, router_acc = loop_state
        micro_index = step_index - (section_count - 1 - section_index)
        is_valid = jnp.logical_and(micro_index >= 0, micro_index < microbatch_count)
        picked = jnp.clip(micro_index, 0, microbatch_count - 1)
        last_grad = lax.dynamic_index_in_dim(out_grad, picked, 0, keepdims=False)
        grad_out = jnp.where(section_index == section_count - 1, last_grad, incoming)
        inputs_now = lax.dynamic_index_in_dim(section_acts, picked, 0, keepdims=False)
        ids_now = lax.dynamic_index_in_dim(section_ids, picked, 0, keepdims=False)
        slots_now = lax.dynamic_index_in_dim(section_slots, picked, 0, keepdims=False)
        caps_now = lax.dynamic_index_in_dim(section_caps, picked, 0, keepdims=False)
        expert_unit_rows, inverse_deviation, normed, logits = token_forward(
            inputs_now, norm_scale_weight, router_w
        )
        pick_bool = ids_now[:, :, None] == columns
        pick_table = pick_bool.astype(jnp.float32)
        chosen = jnp.sum(pick_table * logits[:, None, :], axis=2)
        gate_vals = gate_pair(chosen)
        cap_sel = jnp.sum(jnp.where(pick_bool, caps_now, 0), axis=2)
        kept_mask = slots_now < cap_sel
        target = jnp.where(kept_mask, ids_now * cap_slots + slots_now, -1)
        send_map = jnp.any(positions[:, None, None] == target[None, :, :], axis=2).astype(
            jnp.bfloat16
        )
        sent_u = (
            jnp.dot(send_map, normed, preferred_element_type=jnp.float32)
            .astype(jnp.bfloat16)
            .reshape(experts, cap_slots, model_width)
        )
        sent_grad = (
            jnp.dot(send_map, grad_out, preferred_element_type=jnp.float32)
            .astype(jnp.bfloat16)
            .reshape(experts, cap_slots, model_width)
        )
        recv_u, recv_grad = (
            lax.all_to_all(sent_u, "expert", split_axis=0, concat_axis=0, tiled=True),
            lax.all_to_all(sent_grad, "expert", split_axis=0, concat_axis=0, tiled=True),
        )
        both_u, both_grad = (
            lax.all_gather(recv_u, "dp", axis=0, tiled=True),
            lax.all_gather(recv_grad, "dp", axis=0, tiled=True),
        )
        slot_part, gate_part = run_experts(both_u, both_grad, is_valid)
        summed_u, summed_g = (
            lax.psum_scatter(slot_part, "dp", scatter_dimension=0, tiled=True),
            lax.psum_scatter(gate_part, "dp", scatter_dimension=0, tiled=True),
        )
        ret_u, ret_g = (
            lax.all_to_all(
                summed_u.astype(jnp.bfloat16), "expert", split_axis=0, concat_axis=0, tiled=True
            ),
            lax.all_to_all(
                summed_g.astype(jnp.bfloat16), "expert", split_axis=0, concat_axis=0, tiled=True
            ),
        )
        flat_ret = ret_u.reshape(slot_count, model_width).astype(jnp.float32)
        flat_gate = ret_g.reshape(slot_count).astype(jnp.float32)
        hit_table = (target[:, :, None] == positions).astype(jnp.float32)
        mix_table = jnp.sum(hit_table * gate_vals[:, :, None], axis=1)
        expert_part = jnp.dot(mix_table, flat_ret, precision=PRECISE)
        gate_dots = jnp.sum(hit_table * flat_gate, axis=2)
        in_grad, gain_term, router_term = token_backward(
            grad_out,
            expert_unit_rows,
            inverse_deviation,
            normed,
            norm_scale_weight,
            router_w,
            gate_vals,
            pick_table,
            gate_dots,
            expert_part,
        )
        grads_acc = jnp.where(
            is_valid, lax.dynamic_update_index_in_dim(grads_acc, in_grad, picked, 0), grads_acc
        )
        gain_acc = gain_acc + jnp.where(is_valid, gain_term, 0.0)
        router_acc = router_acc + jnp.where(is_valid, router_term, 0.0)
        outgoing = from_behind(in_grad, "section", -1)
        return (outgoing, grads_acc, gain_acc, router_acc)

    start_state = (
        jnp.zeros((tok_rows, model_width), jnp.bfloat16),
        jnp.zeros((microbatch_count, tok_rows, model_width), jnp.bfloat16),
        jnp.zeros((model_width,), jnp.float32),
        jnp.zeros((model_width, experts), jnp.float32),
    )
    final_state = lax.fori_loop(0, microbatch_count + section_count - 1, step_fn, start_state)
    grads_acc = final_state[1]
    gain_acc, router_acc = (
        lax.psum(final_state[2].astype(jnp.bfloat16), ("expert", "dp")).astype(jnp.float32),
        lax.psum(final_state[3].astype(jnp.bfloat16), ("expert", "dp")).astype(jnp.float32),
    )
    return (grads_acc[None], (gain_acc * grad_scale)[None], (router_acc * grad_scale)[None])


def solution(mesh):
    return jax.shard_map(
        per_device,
        mesh=mesh,
        in_specs=(
            P("section", None, ("expert", "dp"), None),
            P(None, ("expert", "dp"), None),
            P("section", None),
            P("section", None, None),
            P("section", "expert", None, "dp"),
            P("section", "expert", "dp", None),
            P("section", None, ("expert", "dp"), None),
            P("section", None, ("expert", "dp"), None),
            P("section", None, None),
        ),
        out_specs=(
            P("section", None, ("expert", "dp"), None),
            P("section", None),
            P("section", None, None),
        ),
        check_vma=False,
    )
```

profile of v0, /device:TPU:96, one launch (start us, length us, event | category | flops | bytes accessed | tf_op | source)
XLA Modules:
  0.0 1215.3 jit_solution(11664580615775685706)
XLA Ops:
  7.9 1075.4 %while.23 = (s32[]{:T(128)}, bf16[64,1024]{1,0:T(8,128)(2,1)S(1)}, bf16[3,64,1024]{2,1,0:T(8,128)(2,1)S(1)}, f32[1024]{0:T(1024)S(1)}, f32[1024,16]{0,1:T(8,128)...) while((s32[]{:T(128)}, bf16[64,1024]{1,0:T(8,128)(2,1)S(1)}, ...), condition=%wide.region_16.17_spmd.clone.clone, body=%wide.region_0.16_spmd.clone.clone.sunk | while | flops 4244209152 | bytes 89025160 | solution.py:216
  22.2 10.3 all-to-all-done.1
  52.6 21.0 %reduce-scatter.3.cloned.1.call-done = f32[16,10]{1,0:T(8,128)} async-done(((f32[32,10]{1,0:T(8,128)}), f32[16,10]{1,0:T(8,128)}) %reduce-scatter.3.cloned.1.call-update) | async-done | bytes 656 | tf_op jit(solution)/shard_map/while/body/eval_jaxpr/reduce_scatter | solution.py:174
  101.9 11.4 all-to-all-done.3
  161.5 19.3 %reduce-scatter.3.cloned.1.call-done = f32[16,10]{1,0:T(8,128)} async-done(((f32[32,10]{1,0:T(8,128)}), f32[16,10]{1,0:T(8,128)}) %reduce-scatter.3.cloned.1.call-update) | async-done | bytes 656 | tf_op jit(solution)/shard_map/while/body/eval_jaxpr/reduce_scatter | solution.py:174
  208.9 11.4 all-to-all-done.3
  268.5 20.0 %reduce-scatter.3.cloned.1.call-done = f32[16,10]{1,0:T(8,128)} async-done(((f32[32,10]{1,0:T(8,128)}), f32[16,10]{1,0:T(8,128)}) %reduce-scatter.3.cloned.1.call-update) | async-done | bytes 656 | tf_op jit(solution)/shard_map/while/body/eval_jaxpr/reduce_scatter | solution.py:174
  316.6 11.4 all-to-all-done.3
  376.2 20.8 %reduce-scatter.3.cloned.1.call-done = f32[16,10]{1,0:T(8,128)} async-done(((f32[32,10]{1,0:T(8,128)}), f32[16,10]{1,0:T(8,128)}) %reduce-scatter.3.cloned.1.call-update) | async-done | bytes 656 | tf_op jit(solution)/shard_map/while/body/eval_jaxpr/reduce_scatter | solution.py:174
  425.3 11.4 all-to-all-done.3
  456.3 8.9 all-to-all-done.1
  481.3 14.4 %conditional.4 = (f32[320,1024]{1,0:T(8,128)S(1)}, f32[320]{0:T(512)S(1)}) conditional(s32[]{:T(128)} %convert_element_type.282, () %tuple.80, (bf16[32,10,1024]{2,0,1:T(8,128)(2,1)S(1)}, bf16[2048,1024]{1,0:T(8,128)(2,1)}, bf16[32,10,1024]{2,0,1:T(8,128)(2,1)S(1)}, bf16[1024,2048]{1,0:T(8,128)(2,1)}) %tuple.81), branch_computations={%region_7.7_spmd, %region_8.9_spmd} | conditional | flops 4045537024 | bytes 60818760 | solution.py:123
  533.9 11.4 all-to-all-done.3
  589.9 14.4 %conditional.4 = (f32[320,1024]{1,0:T(8,128)S(1)}, f32[320]{0:T(512)S(1)}) conditional(s32[]{:T(128)} %convert_element_type.282, () %tuple.80, (bf16[32,10,1024]{2,0,1:T(8,128)(2,1)S(1)}, bf16[2048,1024]{1,0:T(8,128)(2,1)}, bf16[32,10,1024]{2,0,1:T(8,128)(2,1)S(1)}, bf16[1024,2048]{1,0:T(8,128)(2,1)}) %tuple.81), branch_computations={%region_7.7_spmd, %region_8.9_spmd} | conditional | flops 4045537024 | bytes 60818760 | solution.py:123
  642.4 11.4 all-to-all-done.3
  698.4 14.4 %conditional.4 = (f32[320,1024]{1,0:T(8,128)S(1)}, f32[320]{0:T(512)S(1)}) conditional(s32[]{:T(128)} %convert_element_type.282, () %tuple.80, (bf16[32,10,1024]{2,0,1:T(8,128)(2,1)S(1)}, bf16[2048,1024]{1,0:T(8,128)(2,1)}, bf16[32,10,1024]{2,0,1:T(8,128)(2,1)S(1)}, bf16[1024,2048]{1,0:T(8,128)(2,1)}) %tuple.81), branch_computations={%region_7.7_spmd, %region_8.9_spmd} | conditional | flops 4045537024 | bytes 60818760 | solution.py:123
  750.0 11.4 all-to-all-done.3
  809.6 17.6 %reduce-scatter.3.cloned.1.call-done = f32[16,10]{1,0:T(8,128)} async-done(((f32[32,10]{1,0:T(8,128)}), f32[16,10]{1,0:T(8,128)}) %reduce-scatter.3.cloned.1.call-update) | async-done | bytes 656 | tf_op jit(solution)/shard_map/while/body/eval_jaxpr/reduce_scatter | solution.py:174
  855.3 11.4 all-to-all-done.3
  914.9 16.6 %reduce-scatter.3.cloned.1.call-done = f32[16,10]{1,0:T(8,128)} async-done(((f32[32,10]{1,0:T(8,128)}), f32[16,10]{1,0:T(8,128)}) %reduce-scatter.3.cloned.1.call-update) | async-done | bytes 656 | tf_op jit(solution)/shard_map/while/body/eval_jaxpr/reduce_scatter | solution.py:174
  959.7 11.4 all-to-all-done.3
  1019.3 15.7 %reduce-scatter.3.cloned.1.call-done = f32[16,10]{1,0:T(8,128)} async-done(((f32[32,10]{1,0:T(8,128)}), f32[16,10]{1,0:T(8,128)}) %reduce-scatter.3.cloned.1.call-update) | async-done | bytes 656 | tf_op jit(solution)/shard_map/while/body/eval_jaxpr/reduce_scatter | solution.py:174
  1063.1 11.4 all-to-all-done.3
  1083.3 123.8 %all-reduce = (bf16[1024]{0:T(1024)(128)(2,1)S(1)}, bf16[1024,16]{0,1:T(8,128)(2,1)S(1)}) all-reduce(bf16[1024]{0:T(1024)(128)(2,1)S(1)} %convert_element_type.153, bf16[1024,16]{0,1:T(8,128)(2,1)S(1)} %convert_element_type.155), channel_id=1, replica_groups=mesh['section'=8,'expert'=16,'dp'=2] {'expert','dp'}, use_global_device_ids=true, to_apply=%region_17.18 | all-reduce | flops 17408 | bytes 69632 | tf_op jit(solution)/shard_map/psum | solution.py:219
  (676 shorter events, 811.1 us)
Async XLA Ops:
  36.1 37.6 %reduce-scatter.3.cloned.1.call-start = ((), (), s32[]{:S(2)}) async-start(), calls=%async_computation.6 | async-start | bytes 24576 | tf_op jit(solution)/shard_map/while/body/eval_jaxpr/reduce_scatter | solution.py:174
  50.0 42.5 %reduce-scatter.5.cloned.1.call-start = ((), (), s32[]{:S(2)}) async-start(), calls=%async_computation.7 | async-start | bytes 3145728 | tf_op jit(solution)/shard_map/while/body/eval_jaxpr/reduce_scatter | solution.py:173
  145.4 35.4 %reduce-scatter.3.cloned.1.call-start = ((), (), s32[]{:S(2)}) async-start(), calls=%async_computation.6 | async-start | bytes 24576 | tf_op jit(solution)/shard_map/while/body/eval_jaxpr/reduce_scatter | solution.py:174
  158.8 40.5 %reduce-scatter.5.cloned.1.call-start = ((), (), s32[]{:S(2)}) async-start(), calls=%async_computation.7 | async-start | bytes 3145728 | tf_op jit(solution)/shard_map/while/body/eval_jaxpr/reduce_scatter | solution.py:173
  201.5 18.8 %all-to-all-start.3 = ((bf16[16,10,1024]{2,1,0:T(8,128)(2,1)}), bf16[16,10,1024]{2,1,0:T(8,128)(2,1)S(1)}, u32[]{:S(2)}, u32[]{:S(2)}) async-start(bf16[16,10,1024]{2,1,0:T(8,128)(2,1)} %convert_element_type.283), calls=%async_computation.5 | async-start | bytes 1048576 | tf_op jit(solution)/shard_map/while/body/eval_jaxpr/all_to_all | solution.py:177
  252.3 36.1 %reduce-scatter.3.cloned.1.call-start = ((), (), s32[]{:S(2)}) async-start(), calls=%async_computation.6 | async-start | bytes 24576 | tf_op jit(solution)/shard_map/while/body/eval_jaxpr/reduce_scatter | solution.py:174
  265.8 41.3 %reduce-scatter.5.cloned.1.call-start = ((), (), s32[]{:S(2)}) async-start(), calls=%async_computation.7 | async-start | bytes 3145728 | tf_op jit(solution)/shard_map/while/body/eval_jaxpr/reduce_scatter | solution.py:173
  360.1 37.0 %reduce-scatter.3.cloned.1.call-start = ((), (), s32[]{:S(2)}) async-start(), calls=%async_computation.6 | async-start | bytes 24576 | tf_op jit(solution)/shard_map/while/body/eval_jaxpr/reduce_scatter | solution.py:174
  373.5 42.3 %reduce-scatter.5.cloned.1.call-start = ((), (), s32[]{:S(2)}) async-start(), calls=%async_computation.7 | async-start | bytes 3145728 | tf_op jit(solution)/shard_map/while/body/eval_jaxpr/reduce_scatter | solution.py:173
  468.8 37.0 %reduce-scatter.3.cloned.1.call-start = ((), (), s32[]{:S(2)}) async-start(), calls=%async_computation.6 | async-start | bytes 24576 | tf_op jit(solution)/shard_map/while/body/eval_jaxpr/reduce_scatter | solution.py:174
  496.4 27.9 %reduce-scatter.5.cloned.1.call-start = ((), (), s32[]{:S(2)}) async-start(), calls=%async_computation.7 | async-start | bytes 3145728 | tf_op jit(solution)/shard_map/while/body/eval_jaxpr/reduce_scatter | solution.py:173
  577.3 37.0 %reduce-scatter.3.cloned.1.call-start = ((), (), s32[]{:S(2)}) async-start(), calls=%async_computation.6 | async-start | bytes 24576 | tf_op jit(solution)/shard_map/while/body/eval_jaxpr/reduce_scatter | solution.py:174
  605.0 27.9 %reduce-scatter.5.cloned.1.call-start = ((), (), s32[]{:S(2)}) async-start(), calls=%async_computation.7 | async-start | bytes 3145728 | tf_op jit(solution)/shard_map/while/body/eval_jaxpr/reduce_scatter | solution.py:173
  635.0 18.8 %all-to-all-start.3 = ((bf16[16,10,1024]{2,1,0:T(8,128)(2,1)}), bf16[16,10,1024]{2,1,0:T(8,128)(2,1)S(1)}, u32[]{:S(2)}, u32[]{:S(2)}) async-start(bf16[16,10,1024]{2,1,0:T(8,128)(2,1)} %convert_element_type.283), calls=%async_computation.5 | async-start | bytes 1048576 | tf_op jit(solution)/shard_map/while/body/eval_jaxpr/all_to_all | solution.py:177
  685.9 36.0 %reduce-scatter.3.cloned.1.call-start = ((), (), s32[]{:S(2)}) async-start(), calls=%async_computation.6 | async-start | bytes 24576 | tf_op jit(solution)/shard_map/while/body/eval_jaxpr/reduce_scatter | solution.py:174
  713.6 26.9 %reduce-scatter.5.cloned.1.call-start = ((), (), s32[]{:S(2)}) async-start(), calls=%async_computation.7 | async-start | bytes 3145728 | tf_op jit(solution)/shard_map/while/body/eval_jaxpr/reduce_scatter | solution.py:173
  793.4 33.8 %reduce-scatter.3.cloned.1.call-start = ((), (), s32[]{:S(2)}) async-start(), calls=%async_computation.6 | async-start | bytes 24576 | tf_op jit(solution)/shard_map/while/body/eval_jaxpr/reduce_scatter | solution.py:174
  806.9 38.9 %reduce-scatter.5.cloned.1.call-start = ((), (), s32[]{:S(2)}) async-start(), calls=%async_computation.7 | async-start | bytes 3145728 | tf_op jit(solution)/shard_map/while/body/eval_jaxpr/reduce_scatter | solution.py:173
  847.9 18.8 %all-to-all-start.3 = ((bf16[16,10,1024]{2,1,0:T(8,128)(2,1)}), bf16[16,10,1024]{2,1,0:T(8,128)(2,1)S(1)}, u32[]{:S(2)}, u32[]{:S(2)}) async-start(bf16[16,10,1024]{2,1,0:T(8,128)(2,1)} %convert_element_type.283), calls=%async_computation.5 | async-start | bytes 1048576 | tf_op jit(solution)/shard_map/while/body/eval_jaxpr/all_to_all | solution.py:177
  898.8 32.8 %reduce-scatter.3.cloned.1.call-start = ((), (), s32[]{:S(2)}) async-start(), calls=%async_computation.6 | async-start | bytes 24576 | tf_op jit(solution)/shard_map/while/body/eval_jaxpr/reduce_scatter | solution.py:174
  912.3 37.9 %reduce-scatter.5.cloned.1.call-start = ((), (), s32[]{:S(2)}) async-start(), calls=%async_computation.7 | async-start | bytes 3145728 | tf_op jit(solution)/shard_map/while/body/eval_jaxpr/reduce_scatter | solution.py:173
  1003.1 31.8 %reduce-scatter.3.cloned.1.call-start = ((), (), s32[]{:S(2)}) async-start(), calls=%async_computation.6 | async-start | bytes 24576 | tf_op jit(solution)/shard_map/while/body/eval_jaxpr/reduce_scatter | solution.py:174
  1016.6 37.0 %reduce-scatter.5.cloned.1.call-start = ((), (), s32[]{:S(2)}) async-start(), calls=%async_computation.7 | async-start | bytes 3145728 | tf_op jit(solution)/shard_map/while/body/eval_jaxpr/reduce_scatter | solution.py:173
  1055.7 18.8 %all-to-all-start.3 = ((bf16[16,10,1024]{2,1,0:T(8,128)(2,1)}), bf16[16,10,1024]{2,1,0:T(8,128)(2,1)S(1)}, u32[]{:S(2)}, u32[]{:S(2)}) async-start(bf16[16,10,1024]{2,1,0:T(8,128)(2,1)} %convert_element_type.283), calls=%async_computation.5 | async-start | bytes 1048576 | tf_op jit(solution)/shard_map/while/body/eval_jaxpr/all_to_all | solution.py:177
  (93 other events, 918.9 us)
Sparse Core Ops, SparseCore 0:
  50.1 23.5 reduce-scatter.2
  76.1 16.2 reduce-scatter.4
  159.0 21.7 reduce-scatter.2
  183.1 16.2 reduce-scatter.4
  265.9 22.5 reduce-scatter.2
  290.8 16.2 reduce-scatter.4
  373.6 23.3 reduce-scatter.2
  399.5 16.2 reduce-scatter.4
  496.6 9.1 reduce-scatter.2
  508.1 16.2 reduce-scatter.4
  605.1 9.1 reduce-scatter.2
  616.6 16.2 reduce-scatter.4
  713.7 8.1 reduce-scatter.2
  724.2 16.2 reduce-scatter.4
  807.0 20.1 reduce-scatter.2
  829.6 16.2 reduce-scatter.4
  912.4 19.1 reduce-scatter.2
  933.9 16.2 reduce-scatter.4
  1016.7 18.1 reduce-scatter.2
  1037.3 16.2 reduce-scatter.4
where the time goes:
time: 1220 us
  waiting for transfers between devices  590 us (48%)
  starting transfers between devices  236 us (19%)
  blocking collectives  169 us (14%)
  other arithmetic  71 us (6%)
  matrix products  66.8 us (5%)
  local copies, waits for them, and re-layouts  65.6 us (5%)
  between operations  14.1 us (1%)
    reduce_scatter x10, waiting for transfers between devices, step_fn(): lax.psum_scatter(gate_part, 'dp', scatter_dimension=0, tiled=True)  150 us
    psum x1, blocking collectives, per_device(): lax.psum(final_state[2].astype(jnp.bfloat16), ('expert', 'dp'))  124 us
    all_to_all x10, waiting for transfers between devices, step_fn(): lax.all_to_all(summed_u.astype(jnp.bfloat16), 'expert', split_axis=0, con...  114 us
    all_to_all x10, waiting for transfers between devices, step_fn(): lax.all_to_all(sent_u, 'expert', split_axis=0, concat_axis=0, tiled=True)  90.5 us
    all_to_all x10, waiting for transfers between devices, step_fn(): lax.all_to_all(sent_grad, 'expert', split_axis=0, concat_axis=0, tiled=True)  76.2 us
    all_to_all x10, waiting for transfers between devices, step_fn(): lax.all_to_all(summed_g.astype(jnp.bfloat16), 'expert', split_axis=0, con...  74.6 us
    all_to_all x10, starting transfers between devices, step_fn(): lax.all_to_all(summed_u.astype(jnp.bfloat16), 'expert', split_axis=0, con...  68.1 us
    all_to_all x10, starting transfers between devices, step_fn(): lax.all_to_all(summed_g.astype(jnp.bfloat16), 'expert', split_axis=0, con...  68.1 us
  transfers between devices with their start and end apart: 70, of which 70 were waited for; matrix products, arithmetic and copies ran while one was open for 5% of the time, Pallas kernels for 0%

commit v1 on v0

--- a/solution.py
+++ b/solution.py
@@ -6,6 +6,12 @@
 
 GELU_C = math.sqrt(2.0 / math.pi)
 PRECISE = lax.Precision.HIGHEST
+
+
+def convert_leaves(own_rows):
+    for ii in ("expert", "dp"):
+        own_rows = lax.psum(own_rows, ii)
+    return own_rows
 
 
 def from_behind(shard, axis, by):
@@ -216,7 +222,7 @@
     final_state = lax.fori_loop(0, microbatch_count + section_count - 1, step_fn, start_state)
     grads_acc = final_state[1]
     gain_acc, router_acc = (
-        lax.psum(final_state[2].astype(jnp.bfloat16), ("expert", "dp")).astype(jnp.float32),
+        convert_leaves(final_state[2].astype(jnp.bfloat16)).astype(jnp.float32),
         lax.psum(final_state[3].astype(jnp.bfloat16), ("expert", "dp")).astype(jnp.float32),
     )
     return (grads_acc[None], (gain_acc * grad_scale)[None], (router_acc * grad_scale)[None])

time: 1220 us -> 1260 us (1.033)
  blocking collectives: 169 us -> 207 us
    psum x1 -> x3, blocking collectives: 124 us -> 162 us  [the longest x1 124 us: per_device(): lax.psum(final_state[3].astype(jnp.bfloat16), ('expert', 'dp'))]
where the time goes in v1:
time: 1260 us; the launch traced here: 1250 us
  waiting for transfers between devices  590 us (47%)
  starting transfers between devices  236 us (19%)
  blocking collectives  207 us (16%)
  other arithmetic  71 us (6%)
  matrix products  66.8 us (5%)
  local copies, waits for them, and re-layouts  65.6 us (5%)
  between operations  14 us (1%)
    reduce_scatter x10, waiting for transfers between devices, step_fn(): lax.psum_scatter(gate_part, 'dp', scatter_dimension=0, tiled=True)  150 us
    psum x1, blocking collectives, per_device(): lax.psum(final_state[3].astype(jnp.bfloat16), ('expert', 'dp'))  124 us
    all_to_all x10, waiting for transfers between devices, step_fn(): lax.all_to_all(summed_u.astype(jnp.bfloat16), 'expert', split_axis=0, con...  114 us
    all_to_all x10, waiting for transfers between devices, step_fn(): lax.all_to_all(sent_u, 'expert', split_axis=0, concat_axis=0, tiled=True)  90.5 us
    all_to_all x10, waiting for transfers between devices, step_fn(): lax.all_to_all(sent_grad, 'expert', split_axis=0, concat_axis=0, tiled=True)  76.2 us
    all_to_all x10, waiting for transfers between devices, step_fn(): lax.all_to_all(summed_g.astype(jnp.bfloat16), 'expert', split_axis=0, con...  74.6 us
    all_to_all x10, starting transfers between devices, step_fn(): lax.all_to_all(summed_u.astype(jnp.bfloat16), 'expert', split_axis=0, con...  68.1 us
    all_to_all x10, starting transfers between devices, step_fn(): lax.all_to_all(summed_g.astype(jnp.bfloat16), 'expert', split_axis=0, con...  68.1 us
  transfers between devices with their start and end apart: 70, of which 70 were waited for; matrix products, arithmetic and copies ran while one was open for 5% of the time, Pallas kernels for 0%

profile of v1, /device:TPU:96, one launch (start us, length us, event | category | flops | bytes accessed | tf_op | source)
XLA Modules:
  0.0 1253.2 jit_solution(2888642034845253042)
XLA Ops:
  7.9 1075.4 %while.23 = (s32[]{:T(128)}, bf16[64,1024]{1,0:T(8,128)(2,1)S(1)}, bf16[3,64,1024]{2,1,0:T(8,128)(2,1)S(1)}, f32[1024]{0:T(1024)S(1)}, f32[1024,16]{0,1:T(8,128)...) while((s32[]{:T(128)}, bf16[64,1024]{1,0:T(8,128)(2,1)S(1)}, ...), condition=%wide.region_16.17_spmd.clone.clone, body=%wide.region_0.16_spmd.clone.clone.sunk | while | flops 4244209152 | bytes 89025160 | solution.py:222
  22.2 10.3 all-to-all-done.1
  52.6 21.0 %reduce-scatter.3.cloned.1.call-done = f32[16,10]{1,0:T(8,128)} async-done(((f32[32,10]{1,0:T(8,128)}), f32[16,10]{1,0:T(8,128)}) %reduce-scatter.3.cloned.1.call-update) | async-done | bytes 656 | tf_op jit(solution)/shard_map/while/body/eval_jaxpr/reduce_scatter | solution.py:180
  101.9 11.4 all-to-all-done.3
  161.5 19.3 %reduce-scatter.3.cloned.1.call-done = f32[16,10]{1,0:T(8,128)} async-done(((f32[32,10]{1,0:T(8,128)}), f32[16,10]{1,0:T(8,128)}) %reduce-scatter.3.cloned.1.call-update) | async-done | bytes 656 | tf_op jit(solution)/shard_map/while/body/eval_jaxpr/reduce_scatter | solution.py:180
  208.9 11.4 all-to-all-done.3
  268.5 20.0 %reduce-scatter.3.cloned.1.call-done = f32[16,10]{1,0:T(8,128)} async-done(((f32[32,10]{1,0:T(8,128)}), f32[16,10]{1,0:T(8,128)}) %reduce-scatter.3.cloned.1.call-update) | async-done | bytes 656 | tf_op jit(solution)/shard_map/while/body/eval_jaxpr/reduce_scatter | solution.py:180
  316.6 11.4 all-to-all-done.3
  376.2 20.8 %reduce-scatter.3.cloned.1.call-done = f32[16,10]{1,0:T(8,128)} async-done(((f32[32,10]{1,0:T(8,128)}), f32[16,10]{1,0:T(8,128)}) %reduce-scatter.3.cloned.1.call-update) | async-done | bytes 656 | tf_op jit(solution)/shard_map/while/body/eval_jaxpr/reduce_scatter | solution.py:180
  425.3 11.4 all-to-all-done.3
  481.3 14.4 %conditional.4 = (f32[320,1024]{1,0:T(8,128)S(1)}, f32[320]{0:T(512)S(1)}) conditional(s32[]{:T(128)} %convert_element_type.282, () %tuple.80, (bf16[32,10,1024]{2,0,1:T(8,128)(2,1)S(1)}, bf16[2048,1024]{1,0:T(8,128)(2,1)}, bf16[32,10,1024]{2,0,1:T(8,128)(2,1)S(1)}, bf16[1024,2048]{1,0:T(8,128)(2,1)}) %tuple.81), branch_computations={%region_7.7_spmd, %region_8.9_spmd} | conditional | flops 4045537024 | bytes 60818760 | solution.py:129
  533.9 11.4 all-to-all-done.3
  589.9 14.4 %conditional.4 = (f32[320,1024]{1,0:T(8,128)S(1)}, f32[320]{0:T(512)S(1)}) conditional(s32[]{:T(128)} %convert_element_type.282, () %tuple.80, (bf16[32,10,1024]{2,0,1:T(8,128)(2,1)S(1)}, bf16[2048,1024]{1,0:T(8,128)(2,1)}, bf16[32,10,1024]{2,0,1:T(8,128)(2,1)S(1)}, bf16[1024,2048]{1,0:T(8,128)(2,1)}) %tuple.81), branch_computations={%region_7.7_spmd, %region_8.9_spmd} | conditional | flops 4045537024 | bytes 60818760 | solution.py:129
  642.4 11.4 all-to-all-done.3
  698.4 14.4 %conditional.4 = (f32[320,1024]{1,0:T(8,128)S(1)}, f32[320]{0:T(512)S(1)}) conditional(s32[]{:T(128)} %convert_element_type.282, () %tuple.80, (bf16[32,10,1024]{2,0,1:T(8,128)(2,1)S(1)}, bf16[2048,1024]{1,0:T(8,128)(2,1)}, bf16[32,10,1024]{2,0,1:T(8,128)(2,1)S(1)}, bf16[1024,2048]{1,0:T(8,128)(2,1)}) %tuple.81), branch_computations={%region_7.7_spmd, %region_8.9_spmd} | conditional | flops 4045537024 | bytes 60818760 | solution.py:129
  750.0 11.4 all-to-all-done.3
  809.6 17.6 %reduce-scatter.3.cloned.1.call-done = f32[16,10]{1,0:T(8,128)} async-done(((f32[32,10]{1,0:T(8,128)}), f32[16,10]{1,0:T(8,128)}) %reduce-scatter.3.cloned.1.call-update) | async-done | bytes 656 | tf_op jit(solution)/shard_map/while/body/eval_jaxpr/reduce_scatter | solution.py:180
  855.3 11.4 all-to-all-done.3
  914.9 16.6 %reduce-scatter.3.cloned.1.call-done = f32[16,10]{1,0:T(8,128)} async-done(((f32[32,10]{1,0:T(8,128)}), f32[16,10]{1,0:T(8,128)}) %reduce-scatter.3.cloned.1.call-update) | async-done | bytes 656 | tf_op jit(solution)/shard_map/while/body/eval_jaxpr/reduce_scatter | solution.py:180
  959.7 11.4 all-to-all-done.3
  1019.3 15.7 %reduce-scatter.3.cloned.1.call-done = f32[16,10]{1,0:T(8,128)} async-done(((f32[32,10]{1,0:T(8,128)}), f32[16,10]{1,0:T(8,128)}) %reduce-scatter.3.cloned.1.call-update) | async-done | bytes 656 | tf_op jit(solution)/shard_map/while/body/eval_jaxpr/reduce_scatter | solution.py:180
  1063.1 11.4 all-to-all-done.3
  1083.3 123.8 %psum.23 = bf16[1024,16]{0,1:T(8,128)(2,1)S(1)} all-reduce(bf16[1024,16]{0,1:T(8,128)(2,1)S(1)} %convert_element_type.155), channel_id=1, replica_groups=mesh['section'=8,'expert'=16,'dp'=2] {'expert','dp'}, use_global_device_ids=true, to_apply=%region_19.20 | all-reduce | flops 16384 | bytes 65536 | tf_op jit(solution)/shard_map/psum | solution.py:226
  1207.8 35.5 %psum.21 = bf16[1024]{0:T(1024)(128)(2,1)S(1)} all-reduce(bf16[1024]{0:T(1024)(128)(2,1)S(1)} %convert_element_type.153), channel_id=1, replica_groups=mesh['section'=8,'expert'=16,'dp'=2] {'expert'}, use_global_device_ids=true, to_apply=%region_17.18 | all-reduce | flops 1024 | bytes 4096 | tf_op jit(solution)/shard_map/psum | solution.py:13
  (678 shorter events, 822.4 us)
Async XLA Ops:
  36.1 37.6 %reduce-scatter.3.cloned.1.call-start = ((), (), s32[]{:S(2)}) async-start(), calls=%async_computation.6 | async-start | bytes 24576 | tf_op jit(solution)/shard_map/while/body/eval_jaxpr/reduce_scatter | solution.py:180
  50.0 42.5 %reduce-scatter.5.cloned.1.call-start = ((), (), s32[]{:S(2)}) async-start(), calls=%async_computation.7 | async-start | bytes 3145728 | tf_op jit(solution)/shard_map/while/body/eval_jaxpr/reduce_scatter | solution.py:179
  145.4 35.4 %reduce-scatter.3.cloned.1.call-start = ((), (), s32[]{:S(2)}) async-start(), calls=%async_computation.6 | async-start | bytes 24576 | tf_op jit(solution)/shard_map/while/body/eval_jaxpr/reduce_scatter | solution.py:180
  158.8 40.5 %reduce-scatter.5.cloned.1.call-start = ((), (), s32[]{:S(2)}) async-start(), calls=%async_computation.7 | async-start | bytes 3145728 | tf_op jit(solution)/shard_map/while/body/eval_jaxpr/reduce_scatter | solution.py:179
  201.5 18.8 %all-to-all-start.3 = ((bf16[16,10,1024]{2,1,0:T(8,128)(2,1)}), bf16[16,10,1024]{2,1,0:T(8,128)(2,1)S(1)}, u32[]{:S(2)}, u32[]{:S(2)}) async-start(bf16[16,10,1024]{2,1,0:T(8,128)(2,1)} %convert_element_type.283), calls=%async_computation.5 | async-start | bytes 1048576 | tf_op jit(solution)/shard_map/while/body/eval_jaxpr/all_to_all | solution.py:183
  252.3 36.1 %reduce-scatter.3.cloned.1.call-start = ((), (), s32[]{:S(2)}) async-start(), calls=%async_computation.6 | async-start | bytes 24576 | tf_op jit(solution)/shard_map/while/body/eval_jaxpr/reduce_scatter | solution.py:180
  265.8 41.3 %reduce-scatter.5.cloned.1.call-start = ((), (), s32[]{:S(2)}) async-start(), calls=%async_computation.7 | async-start | bytes 3145728 | tf_op jit(solution)/shard_map/while/body/eval_jaxpr/reduce_scatter | solution.py:179
  360.1 37.0 %reduce-scatter.3.cloned.1.call-start = ((), (), s32[]{:S(2)}) async-start(), calls=%async_computation.6 | async-start | bytes 24576 | tf_op jit(solution)/shard_map/while/body/eval_jaxpr/reduce_scatter | solution.py:180
  373.5 42.3 %reduce-scatter.5.cloned.1.call-start = ((), (), s32[]{:S(2)}) async-start(), calls=%async_computation.7 | async-start | bytes 3145728 | tf_op jit(solution)/shard_map/while/body/eval_jaxpr/reduce_scatter | solution.py:179
  468.8 37.0 %reduce-scatter.3.cloned.1.call-start = ((), (), s32[]{:S(2)}) async-start(), calls=%async_computation.6 | async-start | bytes 24576 | tf_op jit(solution)/shard_map/while/body/eval_jaxpr/reduce_scatter | solution.py:180
  496.4 27.9 %reduce-scatter.5.cloned.1.call-start = ((), (), s32[]{:S(2)}) async-start(), calls=%async_computation.7 | async-start | bytes 3145728 | tf_op jit(solution)/shard_map/while/body/eval_jaxpr/reduce_scatter | solution.py:179
  577.3 37.0 %reduce-scatter.3.cloned.1.call-start = ((), (), s32[]{:S(2)}) async-start(), calls=%async_computation.6 | async-start | bytes 24576 | tf_op jit(solution)/shard_map/while/body/eval_jaxpr/reduce_scatter | solution.py:180
  605.0 27.9 %reduce-scatter.5.cloned.1.call-start = ((), (), s32[]{:S(2)}) async-start(), calls=%async_computation.7 | async-start | bytes 3145728 | tf_op jit(solution)/shard_map/while/body/eval_jaxpr/reduce_scatter | solution.py:179
  635.0 18.8 %all-to-all-start.3 = ((bf16[16,10,1024]{2,1,0:T(8,128)(2,1)}), bf16[16,10,1024]{2,1,0:T(8,128)(2,1)S(1)}, u32[]{:S(2)}, u32[]{:S(2)}) async-start(bf16[16,10,1024]{2,1,0:T(8,128)(2,1)} %convert_element_type.283), calls=%async_computation.5 | async-start | bytes 1048576 | tf_op jit(solution)/shard_map/while/body/eval_jaxpr/all_to_all | solution.py:183
  685.9 36.0 %reduce-scatter.3.cloned.1.call-start = ((), (), s32[]{:S(2)}) async-start(), calls=%async_computation.6 | async-start | bytes 24576 | tf_op jit(solution)/shard_map/while/body/eval_jaxpr/reduce_scatter | solution.py:180
  713.6 26.9 %reduce-scatter.5.cloned.1.call-start = ((), (), s32[]{:S(2)}) async-start(), calls=%async_computation.7 | async-start | bytes 3145728 | tf_op jit(solution)/shard_map/while/body/eval_jaxpr/reduce_scatter | solution.py:179
  793.4 33.8 %reduce-scatter.3.cloned.1.call-start = ((), (), s32[]{:S(2)}) async-start(), calls=%async_computation.6 | async-start | bytes 24576 | tf_op jit(solution)/shard_map/while/body/eval_jaxpr/reduce_scatter | solution.py:180
  806.9 38.9 %reduce-scatter.5.cloned.1.call-start = ((), (), s32[]{:S(2)}) async-start(), calls=%async_computation.7 | async-start | bytes 3145728 | tf_op jit(solution)/shard_map/while/body/eval_jaxpr/reduce_scatter | solution.py:179
  847.9 18.8 %all-to-all-start.3 = ((bf16[16,10,1024]{2,1,0:T(8,128)(2,1)}), bf16[16,10,1024]{2,1,0:T(8,128)(2,1)S(1)}, u32[]{:S(2)}, u32[]{:S(2)}) async-start(bf16[16,10,1024]{2,1,0:T(8,128)(2,1)} %convert_element_type.283), calls=%async_computation.5 | async-start | bytes 1048576 | tf_op jit(solution)/shard_map/while/body/eval_jaxpr/all_to_all | solution.py:183
  898.8 32.8 %reduce-scatter.3.cloned.1.call-start = ((), (), s32[]{:S(2)}) async-start(), calls=%async_computation.6 | async-start | bytes 24576 | tf_op jit(solution)/shard_map/while/body/eval_jaxpr/reduce_scatter | solution.py:180
  912.3 37.9 %reduce-scatter.5.cloned.1.call-start = ((), (), s32[]{:S(2)}) async-start(), calls=%async_computation.7 | async-start | bytes 3145728 | tf_op jit(solution)/shard_map/while/body/eval_jaxpr/reduce_scatter | solution.py:179
  1003.1 31.8 %reduce-scatter.3.cloned.1.call-start = ((), (), s32[]{:S(2)}) async-start(), calls=%async_computation.6 | async-start | bytes 24576 | tf_op jit(solution)/shard_map/while/body/eval_jaxpr/reduce_scatter | solution.py:180
  1016.6 37.0 %reduce-scatter.5.cloned.1.call-start = ((), (), s32[]{:S(2)}) async-start(), calls=%async_computation.7 | async-start | bytes 3145728 | tf_op jit(solution)/shard_map/while/body/eval_jaxpr/reduce_scatter | solution.py:179
  1055.7 18.8 %all-to-all-start.3 = ((bf16[16,10,1024]{2,1,0:T(8,128)(2,1)}), bf16[16,10,1024]{2,1,0:T(8,128)(2,1)S(1)}, u32[]{:S(2)}, u32[]{:S(2)}) async-start(bf16[16,10,1024]{2,1,0:T(8,128)(2,1)} %convert_element_type.283), calls=%async_computation.5 | async-start | bytes 1048576 | tf_op jit(solution)/shard_map/while/body/eval_jaxpr/all_to_all | solution.py:183
  (93 other events, 956.8 us)
Sparse Core Ops, SparseCore 0:
  50.1 23.5 reduce-scatter.2
  76.1 16.2 reduce-scatter.4
  159.0 21.7 reduce-scatter.2
  183.1 16.2 reduce-scatter.4
  265.9 22.5 reduce-scatter.2
  290.8 16.2 reduce-scatter.4
  373.6 23.3 reduce-scatter.2
  399.5 16.2 reduce-scatter.4
  496.6 9.1 reduce-scatter.2
  508.1 16.2 reduce-scatter.4
  605.1 9.1 reduce-scatter.2
  616.6 16.2 reduce-scatter.4
  713.7 8.1 reduce-scatter.2
  724.2 16.2 reduce-scatter.4
  807.0 20.1 reduce-scatter.2
  829.6 16.2 reduce-scatter.4
  912.4 19.1 reduce-scatter.2
  933.9 16.2 reduce-scatter.4
  1016.7 18.1 reduce-scatter.2
  1037.3 16.2 reduce-scatter.4
